TPU v7x, 256 devices: a whole 4x4x8 slice. The times are simulated.
256 devices in a mesh: dp: 32 (over x_lo, z, core), section: 8 (over y, x_hi).
Axes of the slice: x: 4 (x_hi: 2, x_lo: 2; x = x_hi * 2 + x_lo), y: 4, z: 8, core: 2. Of those that a mesh axis runs over, the one named last changes fastest.
Arguments:
- noise: bfloat16 [128, 64, 1536], P('dp'), may hold values from -6 to 6
- sched_index: int32 [128, 3], P('dp'), may hold values from 0 to 1000, as said below
- text_ids: int32 [128, 77], replicated, may hold values from 0 to 49407
- text_table: bfloat16 [49408, 1536], P('dp'), may hold values from -24 to 24
- time_weight: bfloat16 [256, 1536], replicated, may hold values from -0.375 to 0.375
- block_weight: bfloat16 [8, 1536, 1536], P('section', 'dp'), may hold values from -0.15625 to 0.15625
- block_mod: float32 [8, 3, 1536], P('section'), may hold values from -3 to 3
- student_weight: bfloat16 [1536, 1536], P('dp', 'section'), may hold values from -0.15625 to 0.15625
- student_mod: float32 [3, 1536], replicated, may hold values from -3 to 3
- feature_weight: bfloat16 [1536, 512], P('section'), may hold values from -0.15625 to 0.15625
- lin_weight: float32 [512], replicated, may hold values from 0.01 to 0.1
- token_weight: float32 [8192], P('dp'), may hold values from 0.5 to 2
Outputs:
- teacher_latents: bfloat16 [128, 64, 1536], P('dp')
- student_grad: float32 [1536, 1536], P(None, 'section')
- token_distance: float32 [8192], P(('dp', 'section'))
Inputs may be any that keep to these rules, and one draw needn't show every extreme that they name: `sched_index`: each row falls strictly from left to right, by 62 to 250 a step, and starts at 500 or higher.
All inputs are finite; a program needn't handle non-finite values.
Results may differ from a plain program's by a relative error of at most 0.024.
Values may be sent and summed in bfloat16 or wider, within the bound.
A program may use at most 64 MiB of HBM per device.

v0:
```python
import math
import jax
import jax.numpy as jnp
from jax import lax
from jax.sharding import Mesh
from jax.sharding import PartitionSpec as P

LEVELS = 1000
DP = ("dp_0", "dp_1", "dp_2")
DP_SECTION = ("dp_0", "dp_1", "dp_2", "section")


def in_blocks(x, dim, count):
    shape = x.shape
    blocks = x.reshape(*shape[:dim], count, shape[dim] // count, *shape[dim + 1 :])
    return jnp.moveaxis(blocks, dim, 0)


def summed_on_arrival(x, axis, dim):
    blocks = in_blocks(x, dim, lax.axis_size(axis))
    arrived = lax.all_to_all(blocks, axis, split_axis=0, concat_axis=0, tiled=True)
    return arrived.sum(axis=0)


def from_behind(block, axis, distance):
    devices = range(lax.axis_size(axis))
    route = [((i - distance) % len(devices), i) for i in devices]
    return lax.ppermute(block, axis, route)


def picked(x, axis, root):
    return lax.dynamic_index_in_dim(lax.all_gather(x, axis), root, 0, keepdims=False)


def in_order(blocks, dim):
    blocks = jnp.moveaxis(blocks, 0, dim)
    shape = blocks.shape
    return blocks.reshape(*shape[:dim], shape[dim] * shape[dim + 1], *shape[dim + 2 :])


def from_everyone(x, axis):
    copies = jnp.broadcast_to(x, (lax.axis_size(axis), *x.shape))
    return lax.all_to_all(copies, axis, split_axis=0, concat_axis=0, tiled=True)


def collect(x, axis, dim):
    return in_order(from_everyone(x, axis), dim)


def sum_at_owner(x, axis, dim):
    blocks = in_blocks(x, dim, lax.axis_size(axis))
    arrived = lax.all_to_all(blocks, axis, split_axis=0, concat_axis=0, tiled=True)
    return arrived.astype(jnp.float32).sum(axis=0)


def side_by_side(arrays, axis, dim, along):
    widths = [a.shape[along] for a in arrays]
    both = jnp.concatenate(arrays, axis=along)
    result = sum_at_owner(both, axis, dim)
    return tuple(jnp.split(result, [sum(widths[:k]) for k in range(1, len(widths))], axis=along))


def filled_up(lines, count):
    spare = -len(lines) % count
    return jnp.pad(lines, [(0, spare)] + [(0, 0)] * (lines.ndim - 1))


def gather_axes(x, axes, dim):
    far, near = axes
    initial = from_everyone(x, far)
    blocks = jnp.swapaxes(from_everyone(initial, near), 0, 1)
    return in_order(blocks.reshape(-1, *x.shape), dim)


def summed_rows(x, axes, dim):
    far, near = axes
    own = sum_at_owner(in_blocks(x, dim, lax.axis_size(far)), near, dim + 1)
    return jnp.sum(
        lax.all_to_all(own.astype(jnp.bfloat16), far, 0, 0, tiled=True).astype(jnp.float32), axis=0
    )


def sum_by_parts(x, axes):
    lines = x.reshape(-1, x.shape[-1])
    padded = filled_up(lines, lax.axis_size(axes[0]) * lax.axis_size(axes[1]))
    whole = gather_axes(summed_rows(padded, axes, 0).astype(jnp.bfloat16), axes, 0)
    return lax.slice_in_dim(whole, 0, len(lines)).reshape(x.shape).astype(jnp.float32)


def modulated(hidden_f, cond_vec, gains):
    mean_sq = jnp.mean(hidden_f * hidden_f, axis=-1, keepdims=True)
    normed = hidden_f * lax.rsqrt(mean_sq + 1e-06)
    return normed * (1.0 + cond_vec * gains[0]) + cond_vec * gains[1]


def teacher_block(hidden, weight, gains, cond_vec):
    hidden_f = hidden.astype(jnp.float32)
    inputs = modulated(hidden_f, cond_vec, gains).astype(jnp.bfloat16)
    mixed = jnp.dot(inputs, weight, preferred_element_type=jnp.float32)
    return (hidden_f + (1.0 + cond_vec * gains[2]) * jax.nn.gelu(mixed)).astype(jnp.bfloat16)


def distance(feat_student, feat_teacher, lin_weight):
    relu_s = jax.nn.relu(feat_student)
    relu_t = jax.nn.relu(feat_teacher)
    unit_s = relu_s * lax.rsqrt(jnp.mean(relu_s * relu_s, axis=-1, keepdims=True) + 1e-06)
    unit_t = relu_t * lax.rsqrt(jnp.mean(relu_t * relu_t, axis=-1, keepdims=True) + 1e-06)
    gap = unit_s - unit_t
    return jnp.sum(lin_weight * gap * gap, axis=-1)


def store(buffer, value, valid, slot_id):
    old_value = lax.dynamic_index_in_dim(buffer, slot_id, 0, keepdims=False)
    return lax.dynamic_update_index_in_dim(buffer, jnp.where(valid, value, old_value), slot_id, 0)


def local(
    noise,
    sched_index,
    text_ids,
    text_table,
    time_weight,
    block_weight,
    block_mod,
    student_weight,
    student_mod,
    feature_weight,
    lin_weight,
    token_weight,
):
    batches, tokens, model_width = noise.shape
    steps = sched_index.shape[1] - 1
    sections = lax.axis_size("section")
    own_section = lax.axis_index("section")
    vocab_rows = text_table.shape[0]
    offset = lax.axis_index(DP) * vocab_rows
    text_len = text_ids.shape[1]
    local_ids = text_ids - offset
    vocab_ids = jnp.arange(vocab_rows, dtype=jnp.int32)

    def add_group(group_id, counts):
        id_block = lax.dynamic_slice_in_dim(local_ids, group_id * 7, 7, 1)
        return counts + jnp.sum((id_block[:, :, None] == vocab_ids).astype(jnp.float32), axis=1)

    counts = lax.fori_loop(
        0,
        text_len // 7,
        add_group,
        jnp.zeros((batches * lax.axis_size(DP), vocab_rows), jnp.float32),
    )
    pooled = summed_on_arrival(
        jnp.dot(counts.astype(jnp.bfloat16), text_table, preferred_element_type=jnp.float32)
        / text_len,
        DP,
        0,
    )
    weights = lax.all_gather(block_weight, DP, axis=1, tiled=True)[0]
    section_mod = block_mod[0]
    indices_f = sched_index.astype(jnp.float32)
    half_freq = time_weight.shape[0] // 2
    frequency = jnp.exp(-math.log(10000.0) * jnp.arange(half_freq, dtype=jnp.float32) / half_freq)
    angles = indices_f[:, :, None] * frequency
    embedding = jnp.concatenate([jnp.cos(angles), jnp.sin(angles)], axis=-1).astype(jnp.bfloat16)
    time_embed = jnp.dot(
        embedding.reshape(-1, 2 * half_freq), time_weight, preferred_element_type=jnp.float32
    )
    conditions = jax.nn.silu(
        time_embed.reshape(batches, steps + 1, model_width) + pooled[:, None, :]
    )
    deltas = (indices_f[:, 1:] - indices_f[:, :-1]) / LEVELS
    surplus = max(0, batches - sections)
    period = sections + surplus
    tick_count = steps * sections + batches - 1 + (steps - 1) * surplus
    sender = (own_section + sections - 1) % sections

    def locate(section_at, tick_now):
        active = jnp.zeros((), jnp.bool_)
        slot_id = jnp.zeros((), jnp.int32)
        pass_id = jnp.zeros((), jnp.int32)
        for pass_now in range(steps):
            candidate = tick_now - section_at - pass_now * period
            fits = (candidate >= 0) & (candidate < batches)
            slot_id = jnp.where(fits, candidate, slot_id)
            pass_id = jnp.where(fits, pass_now, pass_id)
            active = active | fits
        return (active, slot_id, pass_id)

    def run_block(active, hidden, cond_vec):
        return lax.cond(
            active,
            lambda hidden_in: teacher_block(hidden_in, weights, section_mod, cond_vec),
            lambda hidden_in: hidden_in,
            hidden,
        )

    def tick_entry(tick_now, buffers):
        arrived, iterates = buffers
        active, slot_id, pass_id = locate(own_section, tick_now)
        hidden = lax.dynamic_index_in_dim(arrived, slot_id, 0, keepdims=False)
        start_x = lax.dynamic_index_in_dim(iterates, slot_id, 0, keepdims=False)
        is_first = own_section == 0
        step_size = deltas[slot_id, jnp.maximum(pass_id - 1, 0)]
        advanced = (start_x.astype(jnp.float32) + step_size * hidden.astype(jnp.float32)).astype(
            jnp.bfloat16
        )
        hidden = jnp.where(is_first & (pass_id >= 1), advanced, hidden)
        iterates = store(iterates, hidden, is_first & active, slot_id)
        result = run_block(active, hidden, conditions[slot_id, pass_id])
        got_hidden = from_behind(result, "section", 1)
        valid, source, unused = locate(sender, tick_now)
        arrived = store(arrived, got_hidden, valid, source)
        return (arrived, iterates)

    arrived, iterates = lax.fori_loop(0, tick_count, tick_entry, (noise, noise))
    latest = (
        iterates.astype(jnp.float32)
        + deltas[:, steps - 1][:, None, None] * arrived.astype(jnp.float32)
    ).astype(jnp.bfloat16)
    root_section = 0
    teacher = picked(latest, "section", root_section)
    col_count = student_weight.shape[1]
    first_col = own_section * col_count
    row_count = batches * tokens
    noise_f = noise.astype(jnp.float32)
    cond_zero = conditions[:, 0][:, None, :]
    time_zero = (indices_f[:, 0] / LEVELS)[:, None, None]
    inputs = (
        modulated(noise_f, cond_zero, student_mod)
        .astype(jnp.bfloat16)
        .reshape(row_count, model_width)
    )
    mixed = jnp.dot(inputs, collect(student_weight, DP, 0), preferred_element_type=jnp.float32)
    z_cols = lax.dynamic_slice_in_dim(noise_f, first_col, col_count, 2).reshape(
        row_count, col_count
    )
    gate_full = 1.0 + cond_zero * student_mod[2]
    gate_rows = jnp.broadcast_to(
        lax.dynamic_slice_in_dim(gate_full, first_col, col_count, 2), (batches, tokens, col_count)
    ).reshape(row_count, col_count)
    t_rows = jnp.broadcast_to(time_zero, (batches, tokens, 1)).reshape(row_count, 1)

    def advance(mixed_in):
        return z_cols - t_rows * (z_cols + gate_rows * jax.nn.gelu(mixed_in))

    moved, pull_back = jax.vjp(advance, mixed)
    feat_student = jnp.dot(
        moved.astype(jnp.bfloat16), feature_weight, preferred_element_type=jnp.float32
    )
    target_cols = lax.dynamic_slice_in_dim(teacher, first_col, col_count, 2).reshape(
        row_count, col_count
    )
    feat_teacher = jnp.dot(target_cols, feature_weight, preferred_element_type=jnp.float32)
    share_rows = row_count // sections
    part_student, part_teacher = side_by_side(
        (feat_student.astype(jnp.bfloat16), feat_teacher.astype(jnp.bfloat16)), "section", 0, 1
    )
    weight_share = lax.dynamic_slice_in_dim(token_weight, own_section * share_rows, share_rows, 0)

    def objective(feat_in):
        token_dist = distance(feat_in, part_teacher, lin_weight)
        return (jnp.sum(weight_share * token_dist), token_dist)

    total, pull_feat, token_distance = jax.vjp(objective, part_student, has_aux=True)
    grad_share = pull_feat(jnp.ones_like(total))[0].astype(jnp.bfloat16)
    grad_feat = collect(grad_share, "section", 0)
    out_grad = lax.dot_general(
        grad_feat, feature_weight, (((1,), (1,)), ((), ())), preferred_element_type=jnp.float32
    )
    mixed_grad = pull_back(out_grad)[0].astype(jnp.bfloat16)
    partial_grad = lax.dot_general(
        inputs, mixed_grad, (((0,), (0,)), ((), ())), preferred_element_type=jnp.float32
    )
    student_grad = sum_by_parts(partial_grad.astype(jnp.bfloat16), (("dp_0", "dp_1"), "dp_2"))
    return (teacher, student_grad, token_distance)


def solution(mesh):
    torus = Mesh(
        mesh.devices.reshape(2, 8, 2, mesh.shape["section"]), ("dp_0", "dp_1", "dp_2", "section")
    )
    in_specs = (
        P(DP, None, None),
        P(DP, None),
        P(),
        P(DP, None),
        P(),
        P("section", DP, None),
        P("section", None, None),
        P(DP, "section"),
        P(),
        P("section", None),
        P(),
        P(DP),
    )
    out_specs = (P(DP, None, None), P(None, "section"), P(DP_SECTION))
    return jax.shard_map(local, mesh=torus, in_specs=in_specs, out_specs=out_specs, check_vma=False)
```

profile of v0, /device:TPU:1, one launch (start us, length us, event | category | flops | bytes accessed | tf_op | source)
XLA Modules:
  0.0 550.5 jit_solution(15804008191292427286)
XLA Ops:
  8.7 10.4 %while.33 = (s32[]{:T(128)}, f32[128,1544]{0,1:T(8,128)S(1)}, s32[128,77]{0,1:T(8,128)S(1)}, s32[]{:T(128)}, s32[]{:T(128)}, /*index=5*/s32[]{:T(128)}, s32[]{:T(128)}) while((s32[]{:T(128)}, f32[128,1544]{0,1:T(8,128)S(1)}, s32[128,77]{0,1:T(8,128)S(1)}, s32[]{:T(128)}, s32[]{:T(128)}, /*index=5*/s32[]{:T(128)}, s32[]{:T(128)}) %tuple.112), condition=%wide.region_2.0_spmd.clone, body=%wide.region_0.0_spmd.clone.sunk | while | flops 4347911 | bytes 3173001 | solution.py:145
  23.5 11.1 %all-to-all-start = ((f32[32,4,1536]{2,1,0:T(4,128)}), f32[32,4,1536]{2,1,0:T(4,128)}, u32[]{:S(2)}, u32[]{:S(2)}) async-start(f32[32,4,1536]{2,1,0:T(4,128)} %reshape.121), calls=%async_computation | async-start | bytes 1572864 | tf_op jit(solution)/shard_map/all_to_all | solution.py:21
  36.3 26.8 %all-to-all-done = f32[32,4,1536]{2,1,0:T(4,128)} async-done(((f32[32,4,1536]{2,1,0:T(4,128)}), f32[32,4,1536]{2,1,0:T(4,128)}, u32[]{:S(2)}, u32[]{:S(2)}) %all-to-all-start) | async-done | bytes 786464 | tf_op jit(solution)/shard_map/all_to_all | solution.py:21
  65.9 24.6 %all-gather.4.cloned.1.call-done = bf16[1,1536,1536]{2,1,0:T(8,128)(2,1)} async-done(((bf16[1,48,1536]{2,1,0:T(8,128)(2,1)}), bf16[1,1536,1536]{2,1,0:T(8,128)(2,1)}) %all-gather.4.cloned.1.call-update) | async-done | bytes 4718608 | tf_op jit(solution)/shard_map/all_gather | solution.py:157
  90.5 258.7 %while.32 = (s32[]{:T(128)}, bf16[4,64,1536]{2,1,0:T(8,128)(2,1)S(1)}, bf16[4,64,1536]{2,1,0:T(8,128)(2,1)S(1)}, s32[]{:T(128)}, s32[]{:T(128)}, /*index=5*/pred...) while((s32[]{:T(128)}, ...), condition=%wide.region_8.9_spmd, body=%wide.region_4.8_spmd.sunk | while | flops 305340000 | bytes 8762968 | solution.py:214
  97.3 9.8 %collective-permute-done = bf16[64,1536]{1,0:T(8,128)(2,1)S(1)} collective-permute-done((bf16[64,1536]{1,0:T(8,128)(2,1)S(1)}, bf16[64,1536]{1,0:T(8,128)(2,1)S(1)}, u32[]{:S(2)}, u32[]{:S(2)}) %collective-permute-start) | collective-permute-done | bytes 196640 | tf_op jit(solution)/shard_map/while/body/eval_jaxpr/ppermute | solution.py:28
  114.8 8.9 %collective-permute-done = bf16[64,1536]{1,0:T(8,128)(2,1)S(1)} collective-permute-done((bf16[64,1536]{1,0:T(8,128)(2,1)S(1)}, bf16[64,1536]{1,0:T(8,128)(2,1)S(1)}, u32[]{:S(2)}, u32[]{:S(2)}) %collective-permute-start) | collective-permute-done | bytes 196640 | tf_op jit(solution)/shard_map/while/body/eval_jaxpr/ppermute | solution.py:28
  131.4 8.1 %collective-permute-done = bf16[64,1536]{1,0:T(8,128)(2,1)S(1)} collective-permute-done((bf16[64,1536]{1,0:T(8,128)(2,1)S(1)}, bf16[64,1536]{1,0:T(8,128)(2,1)S(1)}, u32[]{:S(2)}, u32[]{:S(2)}) %collective-permute-start) | collective-permute-done | bytes 196640 | tf_op jit(solution)/shard_map/while/body/eval_jaxpr/ppermute | solution.py:28
  147.2 8.1 %collective-permute-done = bf16[64,1536]{1,0:T(8,128)(2,1)S(1)} collective-permute-done((bf16[64,1536]{1,0:T(8,128)(2,1)S(1)}, bf16[64,1536]{1,0:T(8,128)(2,1)S(1)}, u32[]{:S(2)}, u32[]{:S(2)}) %collective-permute-start) | collective-permute-done | bytes 196640 | tf_op jit(solution)/shard_map/while/body/eval_jaxpr/ppermute | solution.py:28
  169.2 7.1 %collective-permute-done = bf16[64,1536]{1,0:T(8,128)(2,1)S(1)} collective-permute-done((bf16[64,1536]{1,0:T(8,128)(2,1)S(1)}, bf16[64,1536]{1,0:T(8,128)(2,1)S(1)}, u32[]{:S(2)}, u32[]{:S(2)}) %collective-permute-start) | collective-permute-done | bytes 196640 | tf_op jit(solution)/shard_map/while/body/eval_jaxpr/ppermute | solution.py:28
  180.4 6.4 %collective-permute-done = bf16[64,1536]{1,0:T(8,128)(2,1)S(1)} collective-permute-done((bf16[64,1536]{1,0:T(8,128)(2,1)S(1)}, bf16[64,1536]{1,0:T(8,128)(2,1)S(1)}, u32[]{:S(2)}, u32[]{:S(2)}) %collective-permute-start) | collective-permute-done | bytes 196640 | tf_op jit(solution)/shard_map/while/body/eval_jaxpr/ppermute | solution.py:28
  189.6 7.6 %collective-permute-done = bf16[64,1536]{1,0:T(8,128)(2,1)S(1)} collective-permute-done((bf16[64,1536]{1,0:T(8,128)(2,1)S(1)}, bf16[64,1536]{1,0:T(8,128)(2,1)S(1)}, u32[]{:S(2)}, u32[]{:S(2)}) %collective-permute-start) | collective-permute-done | bytes 196640 | tf_op jit(solution)/shard_map/while/body/eval_jaxpr/ppermute | solution.py:28
  199.5 5.3 conditional.2
  205.0 8.1 %collective-permute-done = bf16[64,1536]{1,0:T(8,128)(2,1)S(1)} collective-permute-done((bf16[64,1536]{1,0:T(8,128)(2,1)S(1)}, bf16[64,1536]{1,0:T(8,128)(2,1)S(1)}, u32[]{:S(2)}, u32[]{:S(2)}) %collective-permute-start) | collective-permute-done | bytes 196640 | tf_op jit(solution)/shard_map/while/body/eval_jaxpr/ppermute | solution.py:28
  215.3 5.3 conditional.2
  220.8 8.1 %collective-permute-done = bf16[64,1536]{1,0:T(8,128)(2,1)S(1)} collective-permute-done((bf16[64,1536]{1,0:T(8,128)(2,1)S(1)}, bf16[64,1536]{1,0:T(8,128)(2,1)S(1)}, u32[]{:S(2)}, u32[]{:S(2)}) %collective-permute-start) | collective-permute-done | bytes 196640 | tf_op jit(solution)/shard_map/while/body/eval_jaxpr/ppermute | solution.py:28
  236.5 8.1 %collective-permute-done = bf16[64,1536]{1,0:T(8,128)(2,1)S(1)} collective-permute-done((bf16[64,1536]{1,0:T(8,128)(2,1)S(1)}, bf16[64,1536]{1,0:T(8,128)(2,1)S(1)}, u32[]{:S(2)}, u32[]{:S(2)}) %collective-permute-start) | collective-permute-done | bytes 196640 | tf_op jit(solution)/shard_map/while/body/eval_jaxpr/ppermute | solution.py:28
  252.3 8.1 %collective-permute-done = bf16[64,1536]{1,0:T(8,128)(2,1)S(1)} collective-permute-done((bf16[64,1536]{1,0:T(8,128)(2,1)S(1)}, bf16[64,1536]{1,0:T(8,128)(2,1)S(1)}, u32[]{:S(2)}, u32[]{:S(2)}) %collective-permute-start) | collective-permute-done | bytes 196640 | tf_op jit(solution)/shard_map/while/body/eval_jaxpr/ppermute | solution.py:28
  275.3 6.1 %collective-permute-done = bf16[64,1536]{1,0:T(8,128)(2,1)S(1)} collective-permute-done((bf16[64,1536]{1,0:T(8,128)(2,1)S(1)}, bf16[64,1536]{1,0:T(8,128)(2,1)S(1)}, u32[]{:S(2)}, u32[]{:S(2)}) %collective-permute-start) | collective-permute-done | bytes 196640 | tf_op jit(solution)/shard_map/while/body/eval_jaxpr/ppermute | solution.py:28
  296.7 5.7 %collective-permute-done = bf16[64,1536]{1,0:T(8,128)(2,1)S(1)} collective-permute-done((bf16[64,1536]{1,0:T(8,128)(2,1)S(1)}, bf16[64,1536]{1,0:T(8,128)(2,1)S(1)}, u32[]{:S(2)}, u32[]{:S(2)}) %collective-permute-start) | collective-permute-done | bytes 196640 | tf_op jit(solution)/shard_map/while/body/eval_jaxpr/ppermute | solution.py:28
  306.0 12.7 %collective-permute-done = bf16[64,1536]{1,0:T(8,128)(2,1)S(1)} collective-permute-done((bf16[64,1536]{1,0:T(8,128)(2,1)S(1)}, bf16[64,1536]{1,0:T(8,128)(2,1)S(1)}, u32[]{:S(2)}, u32[]{:S(2)}) %collective-permute-start) | collective-permute-done | bytes 196640 | tf_op jit(solution)/shard_map/while/body/eval_jaxpr/ppermute | solution.py:28
  321.1 13.0 %collective-permute-done = bf16[64,1536]{1,0:T(8,128)(2,1)S(1)} collective-permute-done((bf16[64,1536]{1,0:T(8,128)(2,1)S(1)}, bf16[64,1536]{1,0:T(8,128)(2,1)S(1)}, u32[]{:S(2)}, u32[]{:S(2)}) %collective-permute-start) | collective-permute-done | bytes 196640 | tf_op jit(solution)/shard_map/while/body/eval_jaxpr/ppermute | solution.py:28
  336.5 11.9 %collective-permute-done = bf16[64,1536]{1,0:T(8,128)(2,1)S(1)} collective-permute-done((bf16[64,1536]{1,0:T(8,128)(2,1)S(1)}, bf16[64,1536]{1,0:T(8,128)(2,1)S(1)}, u32[]{:S(2)}, u32[]{:S(2)}) %collective-permute-start) | collective-permute-done | bytes 196640 | tf_op jit(solution)/shard_map/while/body/eval_jaxpr/ppermute | solution.py:28
  351.4 24.4 %all-to-all-start.1 = ((bf16[32,48,192]{2,1,0:T(8,128)(2,1)}), bf16[32,48,192]{2,1,0:T(8,128)(2,1)S(1)}, u32[]{:S(2)}, u32[]{:S(2)}) async-start(bf16[32,48,192]{2,1,0:T(8,128)(2,1)} %broadcast_in_dim.73), calls=%async_computation.1 | async-start | bytes 1572864 | tf_op jit(solution)/shard_map/all_to_all | solution.py:43
  381.7 15.4 %all-to-all-done.1 = bf16[32,48,192]{2,1,0:T(8,128)(2,1)S(1)} async-done(((bf16[32,48,192]{2,1,0:T(8,128)(2,1)}), bf16[32,48,192]{2,1,0:T(8,128)(2,1)S(1)}, u32[]{:S(2)}, u32[]{:S(2)}) %all-to-all-start.1) | async-done | bytes 589856 | tf_op jit(solution)/shard_map/all_to_all | solution.py:43
  397.9 66.6 %all-gather.6.cloned.1.call-done = bf16[32,64,1536]{2,1,0:T(8,128)(2,1)} async-done(((bf16[4,64,1536]{2,1,0:T(8,128)(2,1)}), bf16[32,64,1536]{2,1,0:T(8,128)(2,1)}) %all-gather.6.cloned.1.call-update) | async-done | bytes 6291472 | tf_op jit(solution)/shard_map/all_gather | solution.py:32
  470.5 10.4 %all-to-all-done.2 = bf16[8,32,1024]{2,1,0:T(8,128)(2,1)S(1)} async-done(((bf16[8,32,1024]{2,1,0:T(8,128)(2,1)}), bf16[8,32,1024]{2,1,0:T(8,128)(2,1)S(1)}, u32[]{:S(2)}, u32[]{:S(2)}) %all-to-all-start.2) | async-done | bytes 524320 | tf_op jit(solution)/shard_map/all_to_all | solution.py:52
  482.0 10.3 %all_to_all.40 = bf16[8,32,512]{2,1,0:T(8,128)(2,1)S(1)} all-to-all(bf16[8,32,512]{2,1,0:T(8,128)(2,1)S(1)} %broadcast_in_dim.76), channel_id=1, replica_groups=mesh['dp_0'=2,'dp_1'=8,'dp_2'=2,'section'=8] {'section'}, dimensions={0} | all-to-all | bytes 524288 | tf_op jit(solution)/shard_map/all_to_all | solution.py:43
  493.3 7.0 %all_to_all.41 = bf16[2,16,48,192]{3,2,1,0:T(8,128)(2,1)S(1)} all-to-all(bf16[2,16,48,192]{3,2,1,0:T(8,128)(2,1)S(1)} %copy.46), channel_id=1, replica_groups=mesh['dp_0'=2,'dp_1'=8,'dp_2'=2,'section'=8] {'dp_2'}, dimensions={0} | all-to-all | bytes 1179648 | tf_op jit(solution)/shard_map/all_to_all | solution.py:52
  500.6 17.8 %all_to_all.42 = bf16[16,48,192]{2,1,0:T(8,128)(2,1)S(1)} all-to-all(bf16[16,48,192]{2,1,0:T(8,128)(2,1)S(1)} %reduce_sum.120), channel_id=1, replica_groups=mesh['dp_0'=2,'dp_1'=8,'dp_2'=2,'section'=8] {'dp_0','dp_1'}, dimensions={0} | all-to-all | bytes 589824 | tf_op jit(solution)/shard_map/all_to_all | solution.py:79
  518.5 16.9 %all_to_all.43 = bf16[16,48,192]{2,1,0:T(8,128)(2,1)S(1)} all-to-all(bf16[16,48,192]{2,1,0:T(8,128)(2,1)S(1)} %broadcast_in_dim.77), channel_id=1, replica_groups=mesh['dp_0'=2,'dp_1'=8,'dp_2'=2,'section'=8] {'dp_0','dp_1'}, dimensions={0} | all-to-all | bytes 589824 | tf_op jit(solution)/shard_map/all_to_all | solution.py:43
  535.5 6.4 %all_to_all.44 = bf16[2,16,48,192]{3,2,1,0:T(8,128)(2,1)S(1)} all-to-all(bf16[2,16,48,192]{3,2,1,0:T(8,128)(2,1)S(1)} %broadcast_in_dim.78), channel_id=1, replica_groups=mesh['dp_0'=2,'dp_1'=8,'dp_2'=2,'section'=8] {'dp_2'}, dimensions={0} | all-to-all | bytes 1179648 | tf_op jit(solution)/shard_map/all_to_all | solution.py:43
  (291 shorter events, 190.3 us)
Async XLA Ops:
  7.2 57.2 %copy-start = (bf16[256,1536]{1,0:T(8,128)(2,1)S(1)}, bf16[256,1536]{1,0:T(8,128)(2,1)}, u32[]{:S(2)}) copy-start(bf16[256,1536]{1,0:T(8,128)(2,1)} %param.22) | copy-start | bytes 2359300
  7.2 83.3 %all-gather.4.cloned.1.call-start = ((), (), s32[]{:S(2)}) async-start(), calls=%async_computation.8 | async-start | bytes 4866048 | tf_op jit(solution)/shard_map/all_gather | solution.py:157
  22.4 12.3 %copy-start.1 = (bf16[4,64,1536]{2,1,0:T(8,128)(2,1)S(1)}, bf16[4,64,1536]{2,1,0:T(8,128)(2,1)}, u32[]{:S(2)}) copy-start(bf16[4,64,1536]{2,1,0:T(8,128)(2,1)} %param.18) | copy-start | bytes 2359300
  23.5 39.6 %all-to-all-start = ((f32[32,4,1536]{2,1,0:T(4,128)}), f32[32,4,1536]{2,1,0:T(4,128)}, u32[]{:S(2)}, u32[]{:S(2)}) async-start(f32[32,4,1536]{2,1,0:T(4,128)} %reshape.121), calls=%async_computation | async-start | bytes 1572864 | tf_op jit(solution)/shard_map/all_to_all | solution.py:21
  34.6 429.8 %all-gather.6.cloned.1.call-start = ((), (), s32[]{:S(2)}) async-start(), calls=%async_computation.9 | async-start | bytes 7077888 | tf_op jit(solution)/shard_map/all_gather | solution.py:32
  34.8 55.7 %copy-start.2 = (bf16[4,64,1536]{2,1,0:T(8,128)(2,1)S(1)}, bf16[4,64,1536]{2,1,0:T(8,128)(2,1)}, u32[]{:S(2)}) copy-start(bf16[4,64,1536]{2,1,0:T(8,128)(2,1)} %param.18) | copy-start | bytes 2359300
  97.2 9.9 %collective-permute-start = (bf16[64,1536]{1,0:T(8,128)(2,1)S(1)}, bf16[64,1536]{1,0:T(8,128)(2,1)S(1)}, u32[]{:S(2)}, u32[]{:S(2)}) collective-permute-start(bf16[64,1536]{1,0:T(8,128)(2,1)S(1)} %get-tuple-element.648), channel_id=1, source_target_pairs={{7,0},{0,1},{1,2},{2,3},{3,4},{4,5},{5,6},{6,7},{15,8},{8,9},{9,10... | collective-permute-start | bytes 589832 | tf_op jit(solution)/shard_map/while/body/eval_jaxpr/ppermute | solution.py:28
  114.7 9.0 %collective-permute-start = (bf16[64,1536]{1,0:T(8,128)(2,1)S(1)}, bf16[64,1536]{1,0:T(8,128)(2,1)S(1)}, u32[]{:S(2)}, u32[]{:S(2)}) collective-permute-start(bf16[64,1536]{1,0:T(8,128)(2,1)S(1)} %get-tuple-element.648), channel_id=1, source_target_pairs={{7,0},{0,1},{1,2},{2,3},{3,4},{4,5},{5,6},{6,7},{15,8},{8,9},{9,10... | collective-permute-start | bytes 589832 | tf_op jit(solution)/shard_map/while/body/eval_jaxpr/ppermute | solution.py:28
  131.2 8.2 %collective-permute-start = (bf16[64,1536]{1,0:T(8,128)(2,1)S(1)}, bf16[64,1536]{1,0:T(8,128)(2,1)S(1)}, u32[]{:S(2)}, u32[]{:S(2)}) collective-permute-start(bf16[64,1536]{1,0:T(8,128)(2,1)S(1)} %get-tuple-element.648), channel_id=1, source_target_pairs={{7,0},{0,1},{1,2},{2,3},{3,4},{4,5},{5,6},{6,7},{15,8},{8,9},{9,10... | collective-permute-start | bytes 589832 | tf_op jit(solution)/shard_map/while/body/eval_jaxpr/ppermute | solution.py:28
  147.0 8.2 %collective-permute-start = (bf16[64,1536]{1,0:T(8,128)(2,1)S(1)}, bf16[64,1536]{1,0:T(8,128)(2,1)S(1)}, u32[]{:S(2)}, u32[]{:S(2)}) collective-permute-start(bf16[64,1536]{1,0:T(8,128)(2,1)S(1)} %get-tuple-element.648), channel_id=1, source_target_pairs={{7,0},{0,1},{1,2},{2,3},{3,4},{4,5},{5,6},{6,7},{15,8},{8,9},{9,10... | collective-permute-start | bytes 589832 | tf_op jit(solution)/shard_map/while/body/eval_jaxpr/ppermute | solution.py:28
  157.5 8.2 %collective-permute-start = (bf16[64,1536]{1,0:T(8,128)(2,1)S(1)}, bf16[64,1536]{1,0:T(8,128)(2,1)S(1)}, u32[]{:S(2)}, u32[]{:S(2)}) collective-permute-start(bf16[64,1536]{1,0:T(8,128)(2,1)S(1)} %get-tuple-element.648), channel_id=1, source_target_pairs={{7,0},{0,1},{1,2},{2,3},{3,4},{4,5},{5,6},{6,7},{15,8},{8,9},{9,10... | collective-permute-start | bytes 589832 | tf_op jit(solution)/shard_map/while/body/eval_jaxpr/ppermute | solution.py:28
  168.0 8.2 %collective-permute-start = (bf16[64,1536]{1,0:T(8,128)(2,1)S(1)}, bf16[64,1536]{1,0:T(8,128)(2,1)S(1)}, u32[]{:S(2)}, u32[]{:S(2)}) collective-permute-start(bf16[64,1536]{1,0:T(8,128)(2,1)S(1)} %get-tuple-element.648), channel_id=1, source_target_pairs={{7,0},{0,1},{1,2},{2,3},{3,4},{4,5},{5,6},{6,7},{15,8},{8,9},{9,10... | collective-permute-start | bytes 589832 | tf_op jit(solution)/shard_map/while/body/eval_jaxpr/ppermute | solution.py:28
  178.5 8.2 %collective-permute-start = (bf16[64,1536]{1,0:T(8,128)(2,1)S(1)}, bf16[64,1536]{1,0:T(8,128)(2,1)S(1)}, u32[]{:S(2)}, u32[]{:S(2)}) collective-permute-start(bf16[64,1536]{1,0:T(8,128)(2,1)S(1)} %get-tuple-element.648), channel_id=1, source_target_pairs={{7,0},{0,1},{1,2},{2,3},{3,4},{4,5},{5,6},{6,7},{15,8},{8,9},{9,10... | collective-permute-start | bytes 589832 | tf_op jit(solution)/shard_map/while/body/eval_jaxpr/ppermute | solution.py:28
  189.0 8.2 %collective-permute-start = (bf16[64,1536]{1,0:T(8,128)(2,1)S(1)}, bf16[64,1536]{1,0:T(8,128)(2,1)S(1)}, u32[]{:S(2)}, u32[]{:S(2)}) collective-permute-start(bf16[64,1536]{1,0:T(8,128)(2,1)S(1)} %get-tuple-element.648), channel_id=1, source_target_pairs={{7,0},{0,1},{1,2},{2,3},{3,4},{4,5},{5,6},{6,7},{15,8},{8,9},{9,10... | collective-permute-start | bytes 589832 | tf_op jit(solution)/shard_map/while/body/eval_jaxpr/ppermute | solution.py:28
  204.8 8.2 %collective-permute-start = (bf16[64,1536]{1,0:T(8,128)(2,1)S(1)}, bf16[64,1536]{1,0:T(8,128)(2,1)S(1)}, u32[]{:S(2)}, u32[]{:S(2)}) collective-permute-start(bf16[64,1536]{1,0:T(8,128)(2,1)S(1)} %get-tuple-element.648), channel_id=1, source_target_pairs={{7,0},{0,1},{1,2},{2,3},{3,4},{4,5},{5,6},{6,7},{15,8},{8,9},{9,10... | collective-permute-start | bytes 589832 | tf_op jit(solution)/shard_map/while/body/eval_jaxpr/ppermute | solution.py:28
  220.6 8.2 %collective-permute-start = (bf16[64,1536]{1,0:T(8,128)(2,1)S(1)}, bf16[64,1536]{1,0:T(8,128)(2,1)S(1)}, u32[]{:S(2)}, u32[]{:S(2)}) collective-permute-start(bf16[64,1536]{1,0:T(8,128)(2,1)S(1)} %get-tuple-element.648), channel_id=1, source_target_pairs={{7,0},{0,1},{1,2},{2,3},{3,4},{4,5},{5,6},{6,7},{15,8},{8,9},{9,10... | collective-permute-start | bytes 589832 | tf_op jit(solution)/shard_map/while/body/eval_jaxpr/ppermute | solution.py:28
  236.4 8.2 %collective-permute-start = (bf16[64,1536]{1,0:T(8,128)(2,1)S(1)}, bf16[64,1536]{1,0:T(8,128)(2,1)S(1)}, u32[]{:S(2)}, u32[]{:S(2)}) collective-permute-start(bf16[64,1536]{1,0:T(8,128)(2,1)S(1)} %get-tuple-element.648), channel_id=1, source_target_pairs={{7,0},{0,1},{1,2},{2,3},{3,4},{4,5},{5,6},{6,7},{15,8},{8,9},{9,10... | collective-permute-start | bytes 589832 | tf_op jit(solution)/shard_map/while/body/eval_jaxpr/ppermute | solution.py:28
  252.2 8.2 %collective-permute-start = (bf16[64,1536]{1,0:T(8,128)(2,1)S(1)}, bf16[64,1536]{1,0:T(8,128)(2,1)S(1)}, u32[]{:S(2)}, u32[]{:S(2)}) collective-permute-start(bf16[64,1536]{1,0:T(8,128)(2,1)S(1)} %get-tuple-element.648), channel_id=1, source_target_pairs={{7,0},{0,1},{1,2},{2,3},{3,4},{4,5},{5,6},{6,7},{15,8},{8,9},{9,10... | collective-permute-start | bytes 589832 | tf_op jit(solution)/shard_map/while/body/eval_jaxpr/ppermute | solution.py:28
  262.7 8.2 %collective-permute-start = (bf16[64,1536]{1,0:T(8,128)(2,1)S(1)}, bf16[64,1536]{1,0:T(8,128)(2,1)S(1)}, u32[]{:S(2)}, u32[]{:S(2)}) collective-permute-start(bf16[64,1536]{1,0:T(8,128)(2,1)S(1)} %get-tuple-element.648), channel_id=1, source_target_pairs={{7,0},{0,1},{1,2},{2,3},{3,4},{4,5},{5,6},{6,7},{15,8},{8,9},{9,10... | collective-permute-start | bytes 589832 | tf_op jit(solution)/shard_map/while/body/eval_jaxpr/ppermute | solution.py:28
  273.2 8.2 %collective-permute-start = (bf16[64,1536]{1,0:T(8,128)(2,1)S(1)}, bf16[64,1536]{1,0:T(8,128)(2,1)S(1)}, u32[]{:S(2)}, u32[]{:S(2)}) collective-permute-start(bf16[64,1536]{1,0:T(8,128)(2,1)S(1)} %get-tuple-element.648), channel_id=1, source_target_pairs={{7,0},{0,1},{1,2},{2,3},{3,4},{4,5},{5,6},{6,7},{15,8},{8,9},{9,10... | collective-permute-start | bytes 589832 | tf_op jit(solution)/shard_map/while/body/eval_jaxpr/ppermute | solution.py:28
  283.7 8.2 %collective-permute-start = (bf16[64,1536]{1,0:T(8,128)(2,1)S(1)}, bf16[64,1536]{1,0:T(8,128)(2,1)S(1)}, u32[]{:S(2)}, u32[]{:S(2)}) collective-permute-start(bf16[64,1536]{1,0:T(8,128)(2,1)S(1)} %get-tuple-element.648), channel_id=1, source_target_pairs={{7,0},{0,1},{1,2},{2,3},{3,4},{4,5},{5,6},{6,7},{15,8},{8,9},{9,10... | collective-permute-start | bytes 589832 | tf_op jit(solution)/shard_map/while/body/eval_jaxpr/ppermute | solution.py:28
  294.2 8.2 %collective-permute-start = (bf16[64,1536]{1,0:T(8,128)(2,1)S(1)}, bf16[64,1536]{1,0:T(8,128)(2,1)S(1)}, u32[]{:S(2)}, u32[]{:S(2)}) collective-permute-start(bf16[64,1536]{1,0:T(8,128)(2,1)S(1)} %get-tuple-element.648), channel_id=1, source_target_pairs={{7,0},{0,1},{1,2},{2,3},{3,4},{4,5},{5,6},{6,7},{15,8},{8,9},{9,10... | collective-permute-start | bytes 589832 | tf_op jit(solution)/shard_map/while/body/eval_jaxpr/ppermute | solution.py:28
  304.7 14.0 %collective-permute-start = (bf16[64,1536]{1,0:T(8,128)(2,1)S(1)}, bf16[64,1536]{1,0:T(8,128)(2,1)S(1)}, u32[]{:S(2)}, u32[]{:S(2)}) collective-permute-start(bf16[64,1536]{1,0:T(8,128)(2,1)S(1)} %get-tuple-element.648), channel_id=1, source_target_pairs={{7,0},{0,1},{1,2},{2,3},{3,4},{4,5},{5,6},{6,7},{15,8},{8,9},{9,10... | collective-permute-start | bytes 589832 | tf_op jit(solution)/shard_map/while/body/eval_jaxpr/ppermute | solution.py:28
  320.9 13.1 %collective-permute-start = (bf16[64,1536]{1,0:T(8,128)(2,1)S(1)}, bf16[64,1536]{1,0:T(8,128)(2,1)S(1)}, u32[]{:S(2)}, u32[]{:S(2)}) collective-permute-start(bf16[64,1536]{1,0:T(8,128)(2,1)S(1)} %get-tuple-element.648), channel_id=1, source_target_pairs={{7,0},{0,1},{1,2},{2,3},{3,4},{4,5},{5,6},{6,7},{15,8},{8,9},{9,10... | collective-permute-start | bytes 589832 | tf_op jit(solution)/shard_map/while/body/eval_jaxpr/ppermute | solution.py:28
  336.4 12.0 %collective-permute-start = (bf16[64,1536]{1,0:T(8,128)(2,1)S(1)}, bf16[64,1536]{1,0:T(8,128)(2,1)S(1)}, u32[]{:S(2)}, u32[]{:S(2)}) collective-permute-start(bf16[64,1536]{1,0:T(8,128)(2,1)S(1)} %get-tuple-element.648), channel_id=1, source_target_pairs={{7,0},{0,1},{1,2},{2,3},{3,4},{4,5},{5,6},{6,7},{15,8},{8,9},{9,10... | collective-permute-start | bytes 589832 | tf_op jit(solution)/shard_map/while/body/eval_jaxpr/ppermute | solution.py:28
  351.4 45.6 %all-to-all-start.1 = ((bf16[32,48,192]{2,1,0:T(8,128)(2,1)}), bf16[32,48,192]{2,1,0:T(8,128)(2,1)S(1)}, u32[]{:S(2)}, u32[]{:S(2)}) async-start(bf16[32,48,192]{2,1,0:T(8,128)(2,1)} %broadcast_in_dim.73), calls=%async_computation.1 | async-start | bytes 1572864 | tf_op jit(solution)/shard_map/all_to_all | solution.py:43
  381.7 15.8 %copy-start.4 = (bf16[192,512]{1,0:T(8,128)(2,1)S(1)}, bf16[192,512]{1,0:T(8,128)(2,1)}, u32[]{:S(2)}) copy-start(bf16[192,512]{1,0:T(8,128)(2,1)} %param.27) | copy-start | bytes 589828
  397.9 67.9 %copy-start.5 = (bf16[192,512]{1,0:T(8,128)(2,1)S(1)}, bf16[192,512]{1,0:T(8,128)(2,1)}, u32[]{:S(2)}) copy-start(bf16[192,512]{1,0:T(8,128)(2,1)} %param.27) | copy-start | bytes 589828
  465.7 15.3 %copy-start.3 = (bf16[4,64,1536]{2,1,0:T(8,128)(2,1)}, bf16[4,64,1536]{2,1,0:T(8,128)(2,1)S(1)}, u32[]{:S(2)}) copy-start(bf16[4,64,1536]{2,1,0:T(8,128)(2,1)S(1)} %slice.46) | copy-start | bytes 2359300
  465.7 4.7 copy-start.12
  466.0 15.1 %copy-start.10 = (f32[512]{0:T(512)S(1)}, f32[512]{0:T(512)}, u32[]{:S(2)}) copy-start(f32[512]{0:T(512)} %param.28) | copy-start | bytes 6148
  466.9 14.0 %all-to-all-start.2 = ((bf16[8,32,1024]{2,1,0:T(8,128)(2,1)}), bf16[8,32,1024]{2,1,0:T(8,128)(2,1)S(1)}, u32[]{:S(2)}, u32[]{:S(2)}) async-start(bf16[8,32,1024]{2,1,0:T(8,128)(2,1)} %bitcast.17), calls=%async_computation.2 | async-start | bytes 1048576 | tf_op jit(solution)/shard_map/all_to_all | solution.py:52
  (5 other events, 4.7 us)
Sparse Core Ops, SparseCore 0:
  9.9 80.5 all-gather.3
  350.6 113.7 all-gather.5
where the time goes:
time: 553 us; the launch traced here: 551 us
  waiting for transfers between devices  296 us (54%)
  starting transfers between devices  59.4 us (11%)
  blocking collectives  58.4 us (11%)
  other arithmetic  50.8 us (9%)
  local copies, waits for them, and re-layouts  36.1 us (7%)
  matrix products  32.4 us (6%)
  between operations  14.5 us (3%)
    ppermute x19, waiting for transfers between devices, from_behind(): return lax.ppermute(block, axis, route)  152 us
    all_gather x1, waiting for transfers between devices, picked(): lax.all_gather(x, axis)  66.6 us
    all_to_all x3, blocking collectives, from_everyone(): return lax.all_to_all(copies, axis, split_axis=0, concat_axis=0, tiled=True)  33.7 us
    dot_general x8, matrix products, teacher_block(): mixed = jnp.dot(inputs, weight, preferred_element_type=jnp.float32)  27.2 us
    all_to_all x1, waiting for transfers between devices, summed_on_arrival(): lax.all_to_all(blocks, axis, split_axis=0, concat_axis=0, tiled=True)  26.8 us
    all_gather x1, waiting for transfers between devices, local(): weights = lax.all_gather(block_weight, DP, axis=1, tiled=True)[0]  24.6 us
    all_to_all x1, starting transfers between devices, from_everyone(): return lax.all_to_all(copies, axis, split_axis=0, concat_axis=0, tiled=True)  24.4 us
    ppermute x19, starting transfers between devices, from_behind(): return lax.ppermute(block, axis, route)  20.4 us
  transfers between devices with their start and end apart: 24, of which 24 were waited for; matrix products, arithmetic and copies ran while one was open for 5% of the time, Pallas kernels for 0%

commit v1 on v0

--- a/solution.py
+++ b/solution.py
@@ -154,7 +154,15 @@
         DP,
         0,
     )
-    weights = lax.all_gather(block_weight, DP, axis=1, tiled=True)[0]
+    weights = jnp.concatenate(
+        jax.lax.all_to_all(
+            jnp.stack([block_weight for _ in range(jax.lax.psum(1, axis_name=DP))]),
+            DP,
+            concat_axis=0,
+            split_axis=0,
+        ),
+        axis=1,
+    )[0]
     section_mod = block_mod[0]
     indices_f = sched_index.astype(jnp.float32)
     half_freq = time_weight.shape[0] // 2

time: 553 us -> 635 us (1.15)
  waiting for transfers between devices: 296 us -> 350 us
  blocking collectives: 58.4 us -> 90.6 us
  starting transfers between devices: 59.4 us -> 52.2 us
    all_to_all x1, waiting for transfers between devices: 26.8 us -> 102 us  [local(): jax.lax.all_to_all(jnp.stack([block_weight for _ in range(jax.lax.psum(1,...]
    all_to_all x0 -> x1, blocking collectives: none -> 32.2 us  [summed_on_arrival(): lax.all_to_all(blocks, axis, split_axis=0, concat_axis=0, tiled=True)]
    all_gather x1 -> x0, waiting for transfers between devices: 24.6 us -> none  [local(): weights = lax.all_gather(block_weight, DP, axis=1, tiled=True)[0]]
  transfers between devices with their start and end apart: 24 -> 23, of which waited for: 24 -> 23; matrix products, arithmetic and copies ran while one was open for 5% -> 2% of each run, Pallas kernels for 0% -> 0%
where the time goes in v1:
time: 635 us; the launch traced here: 632 us
  waiting for transfers between devices  350 us (55%)
  blocking collectives  90.6 us (14%)
  starting transfers between devices  52.2 us (8%)
  other arithmetic  51.6 us (8%)
  local copies, waits for them, and re-layouts  38.2 us (6%)
  matrix products  32.4 us (5%)
  between operations  14.5 us (2%)
    ppermute x19, waiting for transfers between devices, from_behind(): return lax.ppermute(block, axis, route)  156 us
    all_to_all x1, waiting for transfers between devices, local(): jax.lax.all_to_all(jnp.stack([block_weight for _ in range(jax.lax.psum(1,...  102 us
    all_gather x1, waiting for transfers between devices, picked(): lax.all_gather(x, axis)  66.6 us
    all_to_all x3, blocking collectives, from_everyone(): return lax.all_to_all(copies, axis, split_axis=0, concat_axis=0, tiled=True)  33.7 us
    all_to_all x1, blocking collectives, summed_on_arrival(): lax.all_to_all(blocks, axis, split_axis=0, concat_axis=0, tiled=True)  32.2 us
    dot_general x8, matrix products, teacher_block(): mixed = jnp.dot(inputs, weight, preferred_element_type=jnp.float32)  27.2 us
    all_to_all x1, starting transfers between devices, from_everyone(): return lax.all_to_all(copies, axis, split_axis=0, concat_axis=0, tiled=True)  24 us
    all_to_all x1, blocking collectives, summed_rows(): lax.all_to_all(own.astype(jnp.bfloat16), far, 0, 0, tiled=True)  17.7 us
  transfers between devices with their start and end apart: 23, of which 23 were waited for; matrix products, arithmetic and copies ran while one was open for 2% of the time, Pallas kernels for 0%

profile of v1, /device:TPU:1, one launch (start us, length us, event | category | flops | bytes accessed | tf_op | source)
XLA Modules:
  0.0 632.4 jit_solution(9712491576433756895)
XLA Ops:
  8.1 10.4 %while.33 = (s32[]{:T(128)}, f32[128,1544]{0,1:T(8,128)S(1)}, s32[128,77]{0,1:T(8,128)S(1)}, s32[]{:T(128)}, s32[]{:T(128)}, /*index=5*/s32[]{:T(128)}, s32[]{:T(128)}) while((s32[]{:T(128)}, f32[128,1544]{0,1:T(8,128)S(1)}, s32[128,77]{0,1:T(8,128)S(1)}, s32[]{:T(128)}, s32[]{:T(128)}, /*index=5*/s32[]{:T(128)}, s32[]{:T(128)}) %tuple.112), condition=%wide.region_2.0_spmd.clone, body=%wide.region_0.0_spmd.clone.sunk | while | flops 4347911 | bytes 3173001 | solution.py:145
  22.0 32.2 %all_to_all.45 = f32[32,4,1536]{2,1,0:T(4,128)} all-to-all(f32[32,4,1536]{2,1,0:T(4,128)S(1)} %reshape.124), channel_id=1, replica_groups=mesh['dp_0'=2,'dp_1'=8,'dp_2'=2,'section'=8] {'dp_0','dp_1','dp_2'}, dimensions={0} | all-to-all | bytes 1572864 | tf_op jit(solution)/shard_map/all_to_all | solution.py:21
  56.9 6.9 %all-to-all-start.1 = ((bf16[32,1,48,1536]{3,2,1,0:T(8,128)(2,1)}), bf16[32,1,48,1536]{3,2,1,0:T(8,128)(2,1)}, u32[]{:S(2)}, u32[]{:S(2)}) async-start(bf16[32,1,48,1536]{3,2,1,0:T(8,128)(2,1)} %stack.2), calls=%async_computation.1 | async-start | bytes 9437184 | tf_op jit(solution)/shard_map/all_to_all | solution.py:158
  68.3 101.5 %all-to-all-done.1 = bf16[32,1,48,1536]{3,2,1,0:T(8,128)(2,1)} async-done(((bf16[32,1,48,1536]{3,2,1,0:T(8,128)(2,1)}), bf16[32,1,48,1536]{3,2,1,0:T(8,128)(2,1)}, u32[]{:S(2)}, u32[]{:S(2)}) %all-to-all-start.1) | async-done | bytes 4718624 | tf_op jit(solution)/shard_map/all_to_all | solution.py:158
  169.8 261.7 %while.32 = (s32[]{:T(128)}, bf16[4,64,1536]{2,1,0:T(8,128)(2,1)S(1)}, bf16[4,64,1536]{2,1,0:T(8,128)(2,1)S(1)}, s32[]{:T(128)}, s32[]{:T(128)}, /*index=5*/pred...) while((s32[]{:T(128)}, ...), condition=%wide.region_8.9_spmd, body=%wide.region_4.8_spmd.sunk | while | flops 305340000 | bytes 8762968 | solution.py:222
  176.7 8.9 %collective-permute-done = bf16[64,1536]{1,0:T(8,128)(2,1)S(1)} collective-permute-done((bf16[64,1536]{1,0:T(8,128)(2,1)S(1)}, bf16[64,1536]{1,0:T(8,128)(2,1)S(1)}, u32[]{:S(2)}, u32[]{:S(2)}) %collective-permute-start) | collective-permute-done | bytes 196640 | tf_op jit(solution)/shard_map/while/body/eval_jaxpr/ppermute | solution.py:28
  193.3 8.1 %collective-permute-done = bf16[64,1536]{1,0:T(8,128)(2,1)S(1)} collective-permute-done((bf16[64,1536]{1,0:T(8,128)(2,1)S(1)}, bf16[64,1536]{1,0:T(8,128)(2,1)S(1)}, u32[]{:S(2)}, u32[]{:S(2)}) %collective-permute-start) | collective-permute-done | bytes 196640 | tf_op jit(solution)/shard_map/while/body/eval_jaxpr/ppermute | solution.py:28
  203.7 5.3 conditional.2
  209.1 8.1 %collective-permute-done = bf16[64,1536]{1,0:T(8,128)(2,1)S(1)} collective-permute-done((bf16[64,1536]{1,0:T(8,128)(2,1)S(1)}, bf16[64,1536]{1,0:T(8,128)(2,1)S(1)}, u32[]{:S(2)}, u32[]{:S(2)}) %collective-permute-start) | collective-permute-done | bytes 196640 | tf_op jit(solution)/shard_map/while/body/eval_jaxpr/ppermute | solution.py:28
  219.5 5.3 conditional.2
  225.0 8.1 %collective-permute-done = bf16[64,1536]{1,0:T(8,128)(2,1)S(1)} collective-permute-done((bf16[64,1536]{1,0:T(8,128)(2,1)S(1)}, bf16[64,1536]{1,0:T(8,128)(2,1)S(1)}, u32[]{:S(2)}, u32[]{:S(2)}) %collective-permute-start) | collective-permute-done | bytes 196640 | tf_op jit(solution)/shard_map/while/body/eval_jaxpr/ppermute | solution.py:28
  247.1 7.1 %collective-permute-done = bf16[64,1536]{1,0:T(8,128)(2,1)S(1)} collective-permute-done((bf16[64,1536]{1,0:T(8,128)(2,1)S(1)}, bf16[64,1536]{1,0:T(8,128)(2,1)S(1)}, u32[]{:S(2)}, u32[]{:S(2)}) %collective-permute-start) | collective-permute-done | bytes 196640 | tf_op jit(solution)/shard_map/while/body/eval_jaxpr/ppermute | solution.py:28
  258.3 6.4 %collective-permute-done = bf16[64,1536]{1,0:T(8,128)(2,1)S(1)} collective-permute-done((bf16[64,1536]{1,0:T(8,128)(2,1)S(1)}, bf16[64,1536]{1,0:T(8,128)(2,1)S(1)}, u32[]{:S(2)}, u32[]{:S(2)}) %collective-permute-start) | collective-permute-done | bytes 196640 | tf_op jit(solution)/shard_map/while/body/eval_jaxpr/ppermute | solution.py:28
  267.6 7.6 %collective-permute-done = bf16[64,1536]{1,0:T(8,128)(2,1)S(1)} collective-permute-done((bf16[64,1536]{1,0:T(8,128)(2,1)S(1)}, bf16[64,1536]{1,0:T(8,128)(2,1)S(1)}, u32[]{:S(2)}, u32[]{:S(2)}) %collective-permute-start) | collective-permute-done | bytes 196640 | tf_op jit(solution)/shard_map/while/body/eval_jaxpr/ppermute | solution.py:28
  283.0 8.1 %collective-permute-done = bf16[64,1536]{1,0:T(8,128)(2,1)S(1)} collective-permute-done((bf16[64,1536]{1,0:T(8,128)(2,1)S(1)}, bf16[64,1536]{1,0:T(8,128)(2,1)S(1)}, u32[]{:S(2)}, u32[]{:S(2)}) %collective-permute-start) | collective-permute-done | bytes 196640 | tf_op jit(solution)/shard_map/while/body/eval_jaxpr/ppermute | solution.py:28
  298.8 8.1 %collective-permute-done = bf16[64,1536]{1,0:T(8,128)(2,1)S(1)} collective-permute-done((bf16[64,1536]{1,0:T(8,128)(2,1)S(1)}, bf16[64,1536]{1,0:T(8,128)(2,1)S(1)}, u32[]{:S(2)}, u32[]{:S(2)}) %collective-permute-start) | collective-permute-done | bytes 196640 | tf_op jit(solution)/shard_map/while/body/eval_jaxpr/ppermute | solution.py:28
  314.7 8.1 %collective-permute-done = bf16[64,1536]{1,0:T(8,128)(2,1)S(1)} collective-permute-done((bf16[64,1536]{1,0:T(8,128)(2,1)S(1)}, bf16[64,1536]{1,0:T(8,128)(2,1)S(1)}, u32[]{:S(2)}, u32[]{:S(2)}) %collective-permute-start) | collective-permute-done | bytes 196640 | tf_op jit(solution)/shard_map/while/body/eval_jaxpr/ppermute | solution.py:28
  330.5 8.1 %collective-permute-done = bf16[64,1536]{1,0:T(8,128)(2,1)S(1)} collective-permute-done((bf16[64,1536]{1,0:T(8,128)(2,1)S(1)}, bf16[64,1536]{1,0:T(8,128)(2,1)S(1)}, u32[]{:S(2)}, u32[]{:S(2)}) %collective-permute-start) | collective-permute-done | bytes 196640 | tf_op jit(solution)/shard_map/while/body/eval_jaxpr/ppermute | solution.py:28
  363.8 6.4 %collective-permute-done = bf16[64,1536]{1,0:T(8,128)(2,1)S(1)} collective-permute-done((bf16[64,1536]{1,0:T(8,128)(2,1)S(1)}, bf16[64,1536]{1,0:T(8,128)(2,1)S(1)}, u32[]{:S(2)}, u32[]{:S(2)}) %collective-permute-start) | collective-permute-done | bytes 196640 | tf_op jit(solution)/shard_map/while/body/eval_jaxpr/ppermute | solution.py:28
  373.6 7.2 %collective-permute-done = bf16[64,1536]{1,0:T(8,128)(2,1)S(1)} collective-permute-done((bf16[64,1536]{1,0:T(8,128)(2,1)S(1)}, bf16[64,1536]{1,0:T(8,128)(2,1)S(1)}, u32[]{:S(2)}, u32[]{:S(2)}) %collective-permute-start) | collective-permute-done | bytes 196640 | tf_op jit(solution)/shard_map/while/body/eval_jaxpr/ppermute | solution.py:28
  383.8 12.8 %collective-permute-done = bf16[64,1536]{1,0:T(8,128)(2,1)S(1)} collective-permute-done((bf16[64,1536]{1,0:T(8,128)(2,1)S(1)}, bf16[64,1536]{1,0:T(8,128)(2,1)S(1)}, u32[]{:S(2)}, u32[]{:S(2)}) %collective-permute-start) | collective-permute-done | bytes 196640 | tf_op jit(solution)/shard_map/while/body/eval_jaxpr/ppermute | solution.py:28
  399.0 12.8 %collective-permute-done = bf16[64,1536]{1,0:T(8,128)(2,1)S(1)} collective-permute-done((bf16[64,1536]{1,0:T(8,128)(2,1)S(1)}, bf16[64,1536]{1,0:T(8,128)(2,1)S(1)}, u32[]{:S(2)}, u32[]{:S(2)}) %collective-permute-start) | collective-permute-done | bytes 196640 | tf_op jit(solution)/shard_map/while/body/eval_jaxpr/ppermute | solution.py:28
  414.3 16.3 %collective-permute-done = bf16[64,1536]{1,0:T(8,128)(2,1)S(1)} collective-permute-done((bf16[64,1536]{1,0:T(8,128)(2,1)S(1)}, bf16[64,1536]{1,0:T(8,128)(2,1)S(1)}, u32[]{:S(2)}, u32[]{:S(2)}) %collective-permute-start) | collective-permute-done | bytes 196640 | tf_op jit(solution)/shard_map/while/body/eval_jaxpr/ppermute | solution.py:28
  433.7 24.0 %all-to-all-start.2 = ((bf16[32,48,192]{2,1,0:T(8,128)(2,1)}), bf16[32,48,192]{2,1,0:T(8,128)(2,1)S(1)}, u32[]{:S(2)}, u32[]{:S(2)}) async-start(bf16[32,48,192]{2,1,0:T(8,128)(2,1)} %broadcast_in_dim.73), calls=%async_computation.2 | async-start | bytes 1572864 | tf_op jit(solution)/shard_map/all_to_all | solution.py:43
  463.6 15.4 %all-to-all-done.2 = bf16[32,48,192]{2,1,0:T(8,128)(2,1)S(1)} async-done(((bf16[32,48,192]{2,1,0:T(8,128)(2,1)}), bf16[32,48,192]{2,1,0:T(8,128)(2,1)S(1)}, u32[]{:S(2)}, u32[]{:S(2)}) %all-to-all-start.2) | async-done | bytes 589856 | tf_op jit(solution)/shard_map/all_to_all | solution.py:43
  479.8 66.6 %all-gather.3.cloned.1.call-done = bf16[32,64,1536]{2,1,0:T(8,128)(2,1)} async-done(((bf16[4,64,1536]{2,1,0:T(8,128)(2,1)}), bf16[32,64,1536]{2,1,0:T(8,128)(2,1)}) %all-gather.3.cloned.1.call-update) | async-done | bytes 6291472 | tf_op jit(solution)/shard_map/all_gather | solution.py:32
  552.4 10.4 %all-to-all-done.3 = bf16[8,32,1024]{2,1,0:T(8,128)(2,1)S(1)} async-done(((bf16[8,32,1024]{2,1,0:T(8,128)(2,1)}), bf16[8,32,1024]{2,1,0:T(8,128)(2,1)S(1)}, u32[]{:S(2)}, u32[]{:S(2)}) %all-to-all-start.3) | async-done | bytes 524320 | tf_op jit(solution)/shard_map/all_to_all | solution.py:52
  563.8 10.3 %all_to_all.46 = bf16[8,32,512]{2,1,0:T(8,128)(2,1)S(1)} all-to-all(bf16[8,32,512]{2,1,0:T(8,128)(2,1)S(1)} %broadcast_in_dim.76), channel_id=1, replica_groups=mesh['dp_0'=2,'dp_1'=8,'dp_2'=2,'section'=8] {'section'}, dimensions={0} | all-to-all | bytes 524288 | tf_op jit(solution)/shard_map/all_to_all | solution.py:43
  575.2 7.0 %all_to_all.47 = bf16[2,16,48,192]{3,2,1,0:T(8,128)(2,1)S(1)} all-to-all(bf16[2,16,48,192]{3,2,1,0:T(8,128)(2,1)S(1)} %copy.46), channel_id=1, replica_groups=mesh['dp_0'=2,'dp_1'=8,'dp_2'=2,'section'=8] {'dp_2'}, dimensions={0} | all-to-all | bytes 1179648 | tf_op jit(solution)/shard_map/all_to_all | solution.py:52
  582.5 17.7 %all_to_all.48 = bf16[16,48,192]{2,1,0:T(8,128)(2,1)S(1)} all-to-all(bf16[16,48,192]{2,1,0:T(8,128)(2,1)S(1)} %reduce_sum.120), channel_id=1, replica_groups=mesh['dp_0'=2,'dp_1'=8,'dp_2'=2,'section'=8] {'dp_0','dp_1'}, dimensions={0} | all-to-all | bytes 589824 | tf_op jit(solution)/shard_map/all_to_all | solution.py:79
  600.3 16.9 %all_to_all.49 = bf16[16,48,192]{2,1,0:T(8,128)(2,1)S(1)} all-to-all(bf16[16,48,192]{2,1,0:T(8,128)(2,1)S(1)} %broadcast_in_dim.77), channel_id=1, replica_groups=mesh['dp_0'=2,'dp_1'=8,'dp_2'=2,'section'=8] {'dp_0','dp_1'}, dimensions={0} | all-to-all | bytes 589824 | tf_op jit(solution)/shard_map/all_to_all | solution.py:43
  617.3 6.4 %all_to_all.50 = bf16[2,16,48,192]{3,2,1,0:T(8,128)(2,1)S(1)} all-to-all(bf16[2,16,48,192]{3,2,1,0:T(8,128)(2,1)S(1)} %broadcast_in_dim.78), channel_id=1, replica_groups=mesh['dp_0'=2,'dp_1'=8,'dp_2'=2,'section'=8] {'dp_2'}, dimensions={0} | all-to-all | bytes 1179648 | tf_op jit(solution)/shard_map/all_to_all | solution.py:43
  (292 shorter events, 190.0 us)
Async XLA Ops:
  7.2 59.5 %copy-start = (bf16[256,1536]{1,0:T(8,128)(2,1)S(1)}, bf16[256,1536]{1,0:T(8,128)(2,1)}, u32[]{:S(2)}) copy-start(bf16[256,1536]{1,0:T(8,128)(2,1)} %param.22) | copy-start | bytes 2359300
  21.7 32.5 %copy-start.6 = (bf16[1,48,1536]{2,1,0:T(8,128)(2,1)S(1)}, bf16[1,48,1536]{2,1,0:T(8,128)(2,1)}, u32[]{:S(2)}) copy-start(bf16[1,48,1536]{2,1,0:T(8,128)(2,1)} %param.23) | copy-start | bytes 442372
  56.9 7.0 %copy-start.1 = (bf16[4,64,1536]{2,1,0:T(8,128)(2,1)S(1)}, bf16[4,64,1536]{2,1,0:T(8,128)(2,1)}, u32[]{:S(2)}) copy-start(bf16[4,64,1536]{2,1,0:T(8,128)(2,1)} %param.18) | copy-start | bytes 2359300
  56.9 112.9 %all-to-all-start.1 = ((bf16[32,1,48,1536]{3,2,1,0:T(8,128)(2,1)}), bf16[32,1,48,1536]{3,2,1,0:T(8,128)(2,1)}, u32[]{:S(2)}, u32[]{:S(2)}) async-start(bf16[32,1,48,1536]{3,2,1,0:T(8,128)(2,1)} %stack.2), calls=%async_computation.1 | async-start | bytes 9437184 | tf_op jit(solution)/shard_map/all_to_all | solution.py:158
  63.8 482.6 %all-gather.3.cloned.1.call-start = ((), (), s32[]{:S(2)}) async-start(), calls=%async_computation.9 | async-start | bytes 7077888 | tf_op jit(solution)/shard_map/all_gather | solution.py:32
  64.0 105.8 %copy-start.2 = (bf16[4,64,1536]{2,1,0:T(8,128)(2,1)S(1)}, bf16[4,64,1536]{2,1,0:T(8,128)(2,1)}, u32[]{:S(2)}) copy-start(bf16[4,64,1536]{2,1,0:T(8,128)(2,1)} %param.18) | copy-start | bytes 2359300
  176.5 9.0 %collective-permute-start = (bf16[64,1536]{1,0:T(8,128)(2,1)S(1)}, bf16[64,1536]{1,0:T(8,128)(2,1)S(1)}, u32[]{:S(2)}, u32[]{:S(2)}) collective-permute-start(bf16[64,1536]{1,0:T(8,128)(2,1)S(1)} %get-tuple-element.648), channel_id=1, source_target_pairs={{7,0},{0,1},{1,2},{2,3},{3,4},{4,5},{5,6},{6,7},{15,8},{8,9},{9,10... | collective-permute-start | bytes 589832 | tf_op jit(solution)/shard_map/while/body/eval_jaxpr/ppermute | solution.py:28
  193.1 8.2 %collective-permute-start = (bf16[64,1536]{1,0:T(8,128)(2,1)S(1)}, bf16[64,1536]{1,0:T(8,128)(2,1)S(1)}, u32[]{:S(2)}, u32[]{:S(2)}) collective-permute-start(bf16[64,1536]{1,0:T(8,128)(2,1)S(1)} %get-tuple-element.648), channel_id=1, source_target_pairs={{7,0},{0,1},{1,2},{2,3},{3,4},{4,5},{5,6},{6,7},{15,8},{8,9},{9,10... | collective-permute-start | bytes 589832 | tf_op jit(solution)/shard_map/while/body/eval_jaxpr/ppermute | solution.py:28
  209.0 8.2 %collective-permute-start = (bf16[64,1536]{1,0:T(8,128)(2,1)S(1)}, bf16[64,1536]{1,0:T(8,128)(2,1)S(1)}, u32[]{:S(2)}, u32[]{:S(2)}) collective-permute-start(bf16[64,1536]{1,0:T(8,128)(2,1)S(1)} %get-tuple-element.648), channel_id=1, source_target_pairs={{7,0},{0,1},{1,2},{2,3},{3,4},{4,5},{5,6},{6,7},{15,8},{8,9},{9,10... | collective-permute-start | bytes 589832 | tf_op jit(solution)/shard_map/while/body/eval_jaxpr/ppermute | solution.py:28
  224.8 8.2 %collective-permute-start = (bf16[64,1536]{1,0:T(8,128)(2,1)S(1)}, bf16[64,1536]{1,0:T(8,128)(2,1)S(1)}, u32[]{:S(2)}, u32[]{:S(2)}) collective-permute-start(bf16[64,1536]{1,0:T(8,128)(2,1)S(1)} %get-tuple-element.648), channel_id=1, source_target_pairs={{7,0},{0,1},{1,2},{2,3},{3,4},{4,5},{5,6},{6,7},{15,8},{8,9},{9,10... | collective-permute-start | bytes 589832 | tf_op jit(solution)/shard_map/while/body/eval_jaxpr/ppermute | solution.py:28
  235.4 8.2 %collective-permute-start = (bf16[64,1536]{1,0:T(8,128)(2,1)S(1)}, bf16[64,1536]{1,0:T(8,128)(2,1)S(1)}, u32[]{:S(2)}, u32[]{:S(2)}) collective-permute-start(bf16[64,1536]{1,0:T(8,128)(2,1)S(1)} %get-tuple-element.648), channel_id=1, source_target_pairs={{7,0},{0,1},{1,2},{2,3},{3,4},{4,5},{5,6},{6,7},{15,8},{8,9},{9,10... | collective-permute-start | bytes 589832 | tf_op jit(solution)/shard_map/while/body/eval_jaxpr/ppermute | solution.py:28
  245.9 8.2 %collective-permute-start = (bf16[64,1536]{1,0:T(8,128)(2,1)S(1)}, bf16[64,1536]{1,0:T(8,128)(2,1)S(1)}, u32[]{:S(2)}, u32[]{:S(2)}) collective-permute-start(bf16[64,1536]{1,0:T(8,128)(2,1)S(1)} %get-tuple-element.648), channel_id=1, source_target_pairs={{7,0},{0,1},{1,2},{2,3},{3,4},{4,5},{5,6},{6,7},{15,8},{8,9},{9,10... | collective-permute-start | bytes 589832 | tf_op jit(solution)/shard_map/while/body/eval_jaxpr/ppermute | solution.py:28
  256.5 8.2 %collective-permute-start = (bf16[64,1536]{1,0:T(8,128)(2,1)S(1)}, bf16[64,1536]{1,0:T(8,128)(2,1)S(1)}, u32[]{:S(2)}, u32[]{:S(2)}) collective-permute-start(bf16[64,1536]{1,0:T(8,128)(2,1)S(1)} %get-tuple-element.648), channel_id=1, source_target_pairs={{7,0},{0,1},{1,2},{2,3},{3,4},{4,5},{5,6},{6,7},{15,8},{8,9},{9,10... | collective-permute-start | bytes 589832 | tf_op jit(solution)/shard_map/while/body/eval_jaxpr/ppermute | solution.py:28
  267.0 8.2 %collective-permute-start = (bf16[64,1536]{1,0:T(8,128)(2,1)S(1)}, bf16[64,1536]{1,0:T(8,128)(2,1)S(1)}, u32[]{:S(2)}, u32[]{:S(2)}) collective-permute-start(bf16[64,1536]{1,0:T(8,128)(2,1)S(1)} %get-tuple-element.648), channel_id=1, source_target_pairs={{7,0},{0,1},{1,2},{2,3},{3,4},{4,5},{5,6},{6,7},{15,8},{8,9},{9,10... | collective-permute-start | bytes 589832 | tf_op jit(solution)/shard_map/while/body/eval_jaxpr/ppermute | solution.py:28
  282.8 8.2 %collective-permute-start = (bf16[64,1536]{1,0:T(8,128)(2,1)S(1)}, bf16[64,1536]{1,0:T(8,128)(2,1)S(1)}, u32[]{:S(2)}, u32[]{:S(2)}) collective-permute-start(bf16[64,1536]{1,0:T(8,128)(2,1)S(1)} %get-tuple-element.648), channel_id=1, source_target_pairs={{7,0},{0,1},{1,2},{2,3},{3,4},{4,5},{5,6},{6,7},{15,8},{8,9},{9,10... | collective-permute-start | bytes 589832 | tf_op jit(solution)/shard_map/while/body/eval_jaxpr/ppermute | solution.py:28
  298.7 8.2 %collective-permute-start = (bf16[64,1536]{1,0:T(8,128)(2,1)S(1)}, bf16[64,1536]{1,0:T(8,128)(2,1)S(1)}, u32[]{:S(2)}, u32[]{:S(2)}) collective-permute-start(bf16[64,1536]{1,0:T(8,128)(2,1)S(1)} %get-tuple-element.648), channel_id=1, source_target_pairs={{7,0},{0,1},{1,2},{2,3},{3,4},{4,5},{5,6},{6,7},{15,8},{8,9},{9,10... | collective-permute-start | bytes 589832 | tf_op jit(solution)/shard_map/while/body/eval_jaxpr/ppermute | solution.py:28
  314.5 8.2 %collective-permute-start = (bf16[64,1536]{1,0:T(8,128)(2,1)S(1)}, bf16[64,1536]{1,0:T(8,128)(2,1)S(1)}, u32[]{:S(2)}, u32[]{:S(2)}) collective-permute-start(bf16[64,1536]{1,0:T(8,128)(2,1)S(1)} %get-tuple-element.648), channel_id=1, source_target_pairs={{7,0},{0,1},{1,2},{2,3},{3,4},{4,5},{5,6},{6,7},{15,8},{8,9},{9,10... | collective-permute-start | bytes 589832 | tf_op jit(solution)/shard_map/while/body/eval_jaxpr/ppermute | solution.py:28
  330.3 8.2 %collective-permute-start = (bf16[64,1536]{1,0:T(8,128)(2,1)S(1)}, bf16[64,1536]{1,0:T(8,128)(2,1)S(1)}, u32[]{:S(2)}, u32[]{:S(2)}) collective-permute-start(bf16[64,1536]{1,0:T(8,128)(2,1)S(1)} %get-tuple-element.648), channel_id=1, source_target_pairs={{7,0},{0,1},{1,2},{2,3},{3,4},{4,5},{5,6},{6,7},{15,8},{8,9},{9,10... | collective-permute-start | bytes 589832 | tf_op jit(solution)/shard_map/while/body/eval_jaxpr/ppermute | solution.py:28
  340.9 8.2 %collective-permute-start = (bf16[64,1536]{1,0:T(8,128)(2,1)S(1)}, bf16[64,1536]{1,0:T(8,128)(2,1)S(1)}, u32[]{:S(2)}, u32[]{:S(2)}) collective-permute-start(bf16[64,1536]{1,0:T(8,128)(2,1)S(1)} %get-tuple-element.648), channel_id=1, source_target_pairs={{7,0},{0,1},{1,2},{2,3},{3,4},{4,5},{5,6},{6,7},{15,8},{8,9},{9,10... | collective-permute-start | bytes 589832 | tf_op jit(solution)/shard_map/while/body/eval_jaxpr/ppermute | solution.py:28
  351.4 8.2 %collective-permute-start = (bf16[64,1536]{1,0:T(8,128)(2,1)S(1)}, bf16[64,1536]{1,0:T(8,128)(2,1)S(1)}, u32[]{:S(2)}, u32[]{:S(2)}) collective-permute-start(bf16[64,1536]{1,0:T(8,128)(2,1)S(1)} %get-tuple-element.648), channel_id=1, source_target_pairs={{7,0},{0,1},{1,2},{2,3},{3,4},{4,5},{5,6},{6,7},{15,8},{8,9},{9,10... | collective-permute-start | bytes 589832 | tf_op jit(solution)/shard_map/while/body/eval_jaxpr/ppermute | solution.py:28
  362.0 8.2 %collective-permute-start = (bf16[64,1536]{1,0:T(8,128)(2,1)S(1)}, bf16[64,1536]{1,0:T(8,128)(2,1)S(1)}, u32[]{:S(2)}, u32[]{:S(2)}) collective-permute-start(bf16[64,1536]{1,0:T(8,128)(2,1)S(1)} %get-tuple-element.648), channel_id=1, source_target_pairs={{7,0},{0,1},{1,2},{2,3},{3,4},{4,5},{5,6},{6,7},{15,8},{8,9},{9,10... | collective-permute-start | bytes 589832 | tf_op jit(solution)/shard_map/while/body/eval_jaxpr/ppermute | solution.py:28
  372.5 8.2 %collective-permute-start = (bf16[64,1536]{1,0:T(8,128)(2,1)S(1)}, bf16[64,1536]{1,0:T(8,128)(2,1)S(1)}, u32[]{:S(2)}, u32[]{:S(2)}) collective-permute-start(bf16[64,1536]{1,0:T(8,128)(2,1)S(1)} %get-tuple-element.648), channel_id=1, source_target_pairs={{7,0},{0,1},{1,2},{2,3},{3,4},{4,5},{5,6},{6,7},{15,8},{8,9},{9,10... | collective-permute-start | bytes 589832 | tf_op jit(solution)/shard_map/while/body/eval_jaxpr/ppermute | solution.py:28
  383.1 13.4 %collective-permute-start = (bf16[64,1536]{1,0:T(8,128)(2,1)S(1)}, bf16[64,1536]{1,0:T(8,128)(2,1)S(1)}, u32[]{:S(2)}, u32[]{:S(2)}) collective-permute-start(bf16[64,1536]{1,0:T(8,128)(2,1)S(1)} %get-tuple-element.648), channel_id=1, source_target_pairs={{7,0},{0,1},{1,2},{2,3},{3,4},{4,5},{5,6},{6,7},{15,8},{8,9},{9,10... | collective-permute-start | bytes 589832 | tf_op jit(solution)/shard_map/while/body/eval_jaxpr/ppermute | solution.py:28
  398.9 12.9 %collective-permute-start = (bf16[64,1536]{1,0:T(8,128)(2,1)S(1)}, bf16[64,1536]{1,0:T(8,128)(2,1)S(1)}, u32[]{:S(2)}, u32[]{:S(2)}) collective-permute-start(bf16[64,1536]{1,0:T(8,128)(2,1)S(1)} %get-tuple-element.648), channel_id=1, source_target_pairs={{7,0},{0,1},{1,2},{2,3},{3,4},{4,5},{5,6},{6,7},{15,8},{8,9},{9,10... | collective-permute-start | bytes 589832 | tf_op jit(solution)/shard_map/while/body/eval_jaxpr/ppermute | solution.py:28
  414.2 16.4 %collective-permute-start = (bf16[64,1536]{1,0:T(8,128)(2,1)S(1)}, bf16[64,1536]{1,0:T(8,128)(2,1)S(1)}, u32[]{:S(2)}, u32[]{:S(2)}) collective-permute-start(bf16[64,1536]{1,0:T(8,128)(2,1)S(1)} %get-tuple-element.648), channel_id=1, source_target_pairs={{7,0},{0,1},{1,2},{2,3},{3,4},{4,5},{5,6},{6,7},{15,8},{8,9},{9,10... | collective-permute-start | bytes 589832 | tf_op jit(solution)/shard_map/while/body/eval_jaxpr/ppermute | solution.py:28
  433.7 45.3 %all-to-all-start.2 = ((bf16[32,48,192]{2,1,0:T(8,128)(2,1)}), bf16[32,48,192]{2,1,0:T(8,128)(2,1)S(1)}, u32[]{:S(2)}, u32[]{:S(2)}) async-start(bf16[32,48,192]{2,1,0:T(8,128)(2,1)} %broadcast_in_dim.73), calls=%async_computation.2 | async-start | bytes 1572864 | tf_op jit(solution)/shard_map/all_to_all | solution.py:43
  463.6 15.8 %copy-start.4 = (bf16[192,512]{1,0:T(8,128)(2,1)S(1)}, bf16[192,512]{1,0:T(8,128)(2,1)}, u32[]{:S(2)}) copy-start(bf16[192,512]{1,0:T(8,128)(2,1)} %param.27) | copy-start | bytes 589828
  479.8 67.9 %copy-start.5 = (bf16[192,512]{1,0:T(8,128)(2,1)S(1)}, bf16[192,512]{1,0:T(8,128)(2,1)}, u32[]{:S(2)}) copy-start(bf16[192,512]{1,0:T(8,128)(2,1)} %param.27) | copy-start | bytes 589828
  547.5 15.3 %copy-start.3 = (bf16[4,64,1536]{2,1,0:T(8,128)(2,1)}, bf16[4,64,1536]{2,1,0:T(8,128)(2,1)S(1)}, u32[]{:S(2)}) copy-start(bf16[4,64,1536]{2,1,0:T(8,128)(2,1)S(1)} %slice.46) | copy-start | bytes 2359300
  547.5 4.7 copy-start.13
  547.9 15.1 %copy-start.11 = (f32[512]{0:T(512)S(1)}, f32[512]{0:T(512)}, u32[]{:S(2)}) copy-start(f32[512]{0:T(512)} %param.28) | copy-start | bytes 6148
  548.8 14.0 %all-to-all-start.3 = ((bf16[8,32,1024]{2,1,0:T(8,128)(2,1)}), bf16[8,32,1024]{2,1,0:T(8,128)(2,1)S(1)}, u32[]{:S(2)}, u32[]{:S(2)}) async-start(bf16[8,32,1024]{2,1,0:T(8,128)(2,1)} %bitcast.18), calls=%async_computation.3 | async-start | bytes 1048576 | tf_op jit(solution)/shard_map/all_to_all | solution.py:52
  (5 other events, 4.7 us)
Sparse Core Ops, SparseCore 0:
  432.9 113.4 all-gather.2
